TPU v7x, 32 devices: a whole 2x2x4 slice. The times are simulated.
32 devices in a mesh: group: 2 (over y), dp: 4 (over z), adapter: 4 (over x, core).
Axes of the slice: x: 2, y: 2, z: 4, core: 2. Of those that a mesh axis runs over, the one named last changes fastest.
Arguments:
- layer_activation_matrix: bfloat16 [8192, 5120], P(('group', 'dp', 'adapter')), parts along dimension 0, may hold values from -6 to 6
- loss_sensitivity: bfloat16 [8192, 1024], P(('group', 'dp', 'adapter')), parts along dimension 0, may hold values from -6 to 6
- fixed_projection_matrix: bfloat16 [5120, 1024], P('dp'), may hold values from -0.078125 to 0.078125
- plugin_factor_matrices: bfloat16 [512, 16, 6144], P('adapter', None, 'dp')
- element_slot_position: int32 [8192], P(('group', 'dp', 'adapter')), parts along dimension 0, may hold values from 0 to 511, as said below
- segment_plugin_choice: int32 [128], P(('group', 'dp', 'adapter')), parts along dimension 0, may hold values from 0 to 511, as said below
Outputs:
- input_token_gradient: bfloat16 [8192, 5120], P(('group', 'dp', 'adapter')), parts along dimension 0
- adapter_grad: float32 [1024, 16, 6144], P(('group', 'adapter'), None, 'dp'), parts along dimension 0
There are 2 independent parts, one for each index of `group`. A program takes and returns all parts, laid end to end along the dimension named above; an argument that names none is the same for every part. Nothing has to cross between parts.
Inputs may be any that keep to these rules, and one draw needn't show every extreme that they name: `element_slot_position`: each device's tokens take distinct rows of its 4 blocks of 128 rows; every block holds 1 to 128 tokens, placed in its last rows, and every device has one full block. `segment_plugin_choice`: blocks of one device may name the same adapter.
All inputs are finite; a program needn't handle non-finite values.
Results may differ from a plain program's by a relative error of at most 0.005.
Values may be sent and summed in bfloat16 or wider, within the bound.
A program may use at most 128 MiB of HBM per device.

v0:
```python
import jax
import jax.numpy as jnp
from jax import lax
from jax.sharding import PartitionSpec as P

BLK = 128


adapter_scale = 2.0


def local(
    layer_activation_matrix,
    loss_sensitivity,
    fixed_projection_matrix,
    plugin_factor_matrices,
    element_slot_position,
    segment_plugin_choice,
):
    token_count, model_width = layer_activation_matrix.shape
    block_count = segment_plugin_choice.shape[0]
    plugins_held_count, plugin_inner_dimension, matrix_width_count = plugin_factor_matrices.shape
    data_count = lax.axis_size("dp")
    owner_count = lax.axis_size("adapter")
    owner_index = lax.axis_index("adapter")
    all_blocks = lax.all_gather(segment_plugin_choice, ("dp", "adapter"), axis=0, tiled=True)
    block_grid = all_blocks.reshape(data_count, owner_count, block_count)
    frozen_weight = jnp.einsum(
        "tk,dk->td",
        loss_sensitivity,
        lax.all_gather(fixed_projection_matrix, "dp", axis=0, tiled=True),
        preferred_element_type=jnp.float32,
    ).astype(jnp.bfloat16)
    frozen_weight = lax.optimization_barrier(frozen_weight).astype(jnp.float32)
    held_plugin_catalog = plugin_factor_matrices.reshape(
        plugins_held_count, plugin_inner_dimension * matrix_width_count
    )
    grid = block_grid.reshape(data_count * owner_count, block_count)
    local_ids = grid - owner_index * plugins_held_count
    onehot = (local_ids[..., None] == jnp.arange(plugins_held_count)).astype(jnp.bfloat16)
    selected = jnp.einsum(
        "...a,ac->...c", onehot, held_plugin_catalog, preferred_element_type=jnp.float32
    )
    pieces = selected.astype(jnp.bfloat16).reshape(
        grid.shape + (plugin_inner_dimension, matrix_width_count)
    )
    arrived = lax.all_to_all(pieces, ("dp", "adapter"), split_axis=0, concat_axis=0, tiled=True)
    arrived = arrived.reshape(
        data_count, owner_count, block_count, plugin_inner_dimension, matrix_width_count
    )
    slices = jnp.sum(arrived, axis=1)
    fetched = jnp.transpose(slices, (1, 2, 0, 3)).reshape(
        block_count, plugin_inner_dimension, data_count * matrix_width_count
    )
    down_weight_rows = fetched[:, :, :model_width]
    up_rows = fetched[:, :, model_width:]
    padded = block_count * BLK
    tokens_pad = (
        jnp.zeros((padded, model_width), jnp.bfloat16)
        .at[element_slot_position]
        .set(layer_activation_matrix)
    )
    tokens_pad = tokens_pad.reshape(block_count, BLK, model_width)
    cotangent_pad = (
        jnp.zeros((padded, loss_sensitivity.shape[1]), jnp.bfloat16)
        .at[element_slot_position]
        .set(loss_sensitivity)
    )
    cotangent_pad = cotangent_pad.reshape(block_count, BLK, loss_sensitivity.shape[1])
    low_in = jnp.einsum(
        "bnd,brd->bnr", tokens_pad, down_weight_rows, preferred_element_type=jnp.float32
    ).astype(jnp.bfloat16)
    low_rank_output = jnp.einsum(
        "bnk,brk->bnr", cotangent_pad, up_rows, preferred_element_type=jnp.float32
    ).astype(jnp.bfloat16)
    adapter_input_gradient = jnp.einsum(
        "bnr,brd->bnd", low_rank_output, down_weight_rows, preferred_element_type=jnp.float32
    )
    adapter_input_gradient = adapter_input_gradient.reshape(padded, model_width)[
        element_slot_position
    ]
    input_token_gradient = (frozen_weight + adapter_scale * adapter_input_gradient).astype(
        jnp.bfloat16
    )
    down_gradient = adapter_scale * jnp.einsum(
        "bnr,bnd->brd", low_rank_output, tokens_pad, preferred_element_type=jnp.float32
    )
    up_gradient = adapter_scale * jnp.einsum(
        "bnr,bnk->brk", low_in, cotangent_pad, preferred_element_type=jnp.float32
    )
    block_grads = jnp.concatenate([down_gradient, up_gradient], axis=2)
    sliced = jnp.transpose(
        block_grads.reshape(block_count, plugin_inner_dimension, data_count, matrix_width_count),
        (2, 0, 1, 3),
    )
    received = lax.all_to_all(sliced, "dp", split_axis=0, concat_axis=0, tiled=True)
    everyone = lax.all_gather(received, "adapter", axis=0, tiled=True)
    source_ids = jnp.transpose(block_grid, (1, 0, 2)).reshape(-1)
    local_ids = source_ids - owner_index * plugins_held_count
    valid = (local_ids >= 0) & (local_ids < plugins_held_count)
    target_ids = jnp.where(valid, local_ids, plugins_held_count)
    rows_all = everyone.reshape(source_ids.shape[0], plugin_inner_dimension, matrix_width_count)
    adapter_grad = (
        jnp.zeros((plugins_held_count, plugin_inner_dimension, matrix_width_count), jnp.float32)
        .at[target_ids]
        .add(rows_all, mode="drop")
    )
    return (input_token_gradient, adapter_grad)


def solution(mesh):
    return jax.shard_map(
        local,
        mesh=mesh,
        in_specs=(
            P(("group", "dp", "adapter"), None),
            P(("group", "dp", "adapter"), None),
            P("dp", None),
            P("adapter", None, "dp"),
            P(("group", "dp", "adapter")),
            P(("group", "dp", "adapter")),
        ),
        out_specs=(P(("group", "dp", "adapter"), None), P(("group", "adapter"), None, "dp")),
        check_vma=False,
    )
```

profile of v0, /device:TPU:3, one launch (start us, length us, event | category | flops | bytes accessed | tf_op | source)
XLA Modules:
  0.0 370.5 jit_solution(7839351464214619831)
XLA Ops:
  7.2 0.0 all-gather.3.cloned.1.call-start
  7.2 0.7 all-gather.3.cloned.1.call-update
  7.9 1.2 dynamic-slice
  9.8 0.9 dynamic-update-slice
  10.7 8.9 %all-reduce = s32[64]{0:T(128)S(1)} all-reduce(s32[64]{0:T(128)S(1)} %dynamic-update-slice), channel_id=1, replica_groups=mesh['group'=2,'dp'=4,'adapter'=4] {'dp','adapter'}, use_global_device_ids=true, to_apply=%add | all-reduce | flops 64 | bytes 512
  19.6 0.1 sub.33
  19.7 0.1 copy.14
  19.8 9.2 %reshape.124 = bf16[128,24576,1]{1,0,2:T(8,128)(2,1)} reshape(bf16[128,16,1536]{2,1,0:T(8,128)(2,1)} %param.9) | data formatting | bytes 12582912 | tf_op jit(solution)/shard_map/reshape | solution.py:35
  29.0 3.8 %convolution_convert_fusion = bf16[16,4,24576]{2,0,1:T(8,128)(2,1)S(1)} fusion(bf16[128,24576,1]{1,0,2:T(8,128)(2,1)} %reshape.124, s32[16,4]{0,1:T(4,128)S(1)} %copy.14), kind=kOutput, calls=%fused_computation.4 | convolution fusion | flops 404234240 | bytes 9437440 | tf_op jit(solution)/shard_map/...a,ac->...c/dot_general | solution.py:41
  32.8 1.0 copy.24
  33.8 0.0 copy-start.3
  33.8 2.0 copy.15
  35.9 7.6 %all-to-all-start = ((bf16[16,4,16,1536]{3,2,1,0:T(8,128)(2,1)}), bf16[16,4,16,1536]{3,2,1,0:T(8,128)(2,1)S(1)}, u32[]{:S(2)}, u32[]{:S(2)}) async-start(bf16[16,4,16,1536]{3,2,1,0:T(8,128)(2,1)} %copy.15), calls=%async_computation | async-start | bytes 6291456 | tf_op jit(solution)/shard_map/all_to_all | solution.py:47
  43.5 0.0 all-gather.5.cloned.1.call-start
  43.5 0.0 copy-done.3
  43.6 3.2 scatter_custom_fusion
  46.7 8.5 %scatter_custom_fusion.1 = bf16[512,5120]{1,0:T(8,128)(2,1)} fusion(s32[256]{0:T(256)S(1)} %compare_select_fusion, bf16[256,5120]{1,0:T(8,128)(2,1)} %param.6, bf16[]{:T(256)} %constant.7.clone.1), kind=kCustom, calls=%fused_computation.9 | custom fusion | bytes 5243392 | tf_op jit(solution)/shard_map/scatter | solution.py:61
  55.2 104.9 %all-to-all-done = bf16[16,4,16,1536]{3,2,1,0:T(8,128)(2,1)S(1)} async-done(((bf16[16,4,16,1536]{3,2,1,0:T(8,128)(2,1)}), bf16[16,4,16,1536]{3,2,1,0:T(8,128)(2,1)S(1)}, u32[]{:S(2)}, u32[]{:S(2)}) %all-to-all-start) | async-done | bytes 3145760 | tf_op jit(solution)/shard_map/all_to_all | solution.py:47
  160.1 0.0 copy-start
  160.1 0.6 bitcast_reduce_fusion
  160.7 0.0 copy-start.2
  160.7 0.1 copy.23
  160.8 1.9 convolution_convert_fusion.3
  162.7 0.2 copy-done
  162.9 0.8 convolution_multiply_fusion
  163.7 0.0 copy-done.2
  163.7 4.1 %convolution_multiply_fusion.1 = f32[4,16,1024]{2,1,0:T(8,128)S(1)} fusion(bf16[4,128,1024]{2,1,0:T(8,128)(2,1)S(1)} %bitcast.42, bf16[4,128,5120]{2,1,0:T(8,128)(2,1)} %bitcast.37, bf16[4,16,6144]{2,1,0:T(8,128)(2,1)S(1)} %bitcast.44), kind=kOutput, calls=%fused_computation.13 | convolution fusion | flops 100737024 | bytes 7208960 | tf_op jit(solution)/shard_map/bnr,bnk->brk/dot_general | solution.py:88
  167.8 0.1 pad_maximum_fusion
  168.0 0.1 copy.26
  168.1 107.9 %all_to_all.10 = f32[4,4,16,1536]{3,2,1,0:T(8,128)} all-to-all(f32[4,4,16,1536]{3,2,1,0:T(8,128)S(1)} %bitcast.47), channel_id=1, replica_groups=mesh['group'=2,'dp'=4,'adapter'=4] {'dp'}, dimensions={0} | all-to-all | bytes 3145728 | tf_op jit(solution)/shard_map/all_to_all | solution.py:96
  276.0 0.0 all-gather.5.cloned.1.call-update
  276.0 0.1 sub.34
  276.1 0.1 sub.36
  276.3 5.6 %fusion.4 = f32[4,128,5120]{2,1,0:T(8,128)} fusion(bf16[4,128,16]{1,2,0:T(8,128)(2,1)S(1)} %convolution_convert_fusion.3, bf16[4,16,6144]{2,1,0:T(8,128)(2,1)S(1)} %bitcast.45), kind=kOutput, calls=%fused_computation.17 | convolution fusion | flops 83886080 | bytes 11157504 | tf_op jit(solution)/shard_map/bnr,brd->bnd/dot_general | solution.py:76
  281.9 0.0 copy-start.4
  281.9 10.8 %gather_fusion = f32[256,5120]{1,0:T(8,128)} fusion(f32[512,5120]{1,0:T(8,128)} %bitcast.36, s32[1024]{0:T(1024)S(1)} %pad_clamp_fusion), kind=kCustom, calls=%fused_computation | custom fusion | bytes 10486784 | tf_op jit(solution)/shard_map/gather | solution.py:79
  292.7 3.0 all-gather.3.cloned.1.call-done
  295.7 0.0 copy-done.4
  295.7 0.0 copy-start.1
  295.7 11.3 %convolution_convert_fusion.1 = bf16[256,5120]{1,0:T(8,128)(2,1)S(1)} fusion(bf16[256,1024]{1,0:T(8,128)(2,1)S(1)} %copy-done.4, bf16[5120,1024]{1,0:T(8,128)(2,1)} %all-gather.3.cloned.1.call-done), kind=kOutput, calls=%fused_computation.5 | convolution fusion | flops 2685665280 | bytes 13631488 | tf_op jit(solution)/shard_map/tk,dk->td/dot_general | solution.py:28
  307.0 0.0 copy-done.1
  307.0 2.3 add_convert_fusion
  309.3 31.6 %all-gather.5.cloned.1.call-done = f32[16,4,16,1536]{3,2,1,0:T(8,128)} async-done(((f32[4,4,16,1536]{3,2,1,0:T(8,128)}), f32[16,4,16,1536]{3,2,1,0:T(8,128)}) %all-gather.5.cloned.1.call-update) | async-done | bytes 6291472 | tf_op jit(solution)/shard_map/all_gather | solution.py:97
  340.9 6.4 %broadcast_in_dim.21 = f32[128,16,1536]{2,1,0:T(8,128)} broadcast(f32[]{:T(128)} %constant.13.clone.1), dimensions={} | broadcast | bytes 12582916 | tf_op jit(solution)/shard_map/broadcast_in_dim | solution.py:104
  347.3 16.4 %scatter_fusion = f32[128,16,1536]{2,1,0:T(8,128)} fusion(f32[128,16,1536]{2,1,0:T(8,128)} %broadcast_in_dim.21, s32[64]{0:T(128)S(1)} %fusion.10, f32[64,16,1536]{2,1,0:T(8,128)} %bitcast.48), kind=kCustom, calls=%fused_computation.3 | custom fusion | flops 1572864 | bytes 18874624 | tf_op jit(solution)/shard_map/scatter-add | solution.py:106
  (6 shorter events, 0.0 us)
Async XLA Ops:
  7.2 288.6 %all-gather.3.cloned.1.call-start = ((), (), s32[]{:S(2)}) async-start(), calls=%async_computation.2 | async-start | bytes 13107200 | tf_op jit(solution)/shard_map/all_gather | solution.py:31
  33.8 9.7 %copy-start.3 = (s32[256]{0:T(256)S(1)}, s32[256]{0:T(256)}, u32[]{:S(2)}) copy-start(s32[256]{0:T(256)} %param.10) | copy-start | bytes 3076
  35.9 124.3 %all-to-all-start = ((bf16[16,4,16,1536]{3,2,1,0:T(8,128)(2,1)}), bf16[16,4,16,1536]{3,2,1,0:T(8,128)(2,1)S(1)}, u32[]{:S(2)}, u32[]{:S(2)}) async-start(bf16[16,4,16,1536]{3,2,1,0:T(8,128)(2,1)} %copy.15), calls=%async_computation | async-start | bytes 6291456 | tf_op jit(solution)/shard_map/all_to_all | solution.py:47
  43.5 297.4 %all-gather.5.cloned.1.call-start = ((), (), s32[]{:S(2)}) async-start(), calls=%async_computation.3 | async-start | bytes 7864320 | tf_op jit(solution)/shard_map/all_gather | solution.py:97
  160.1 2.8 copy-start
  160.7 3.0 copy-start.2
  281.9 13.8 %copy-start.4 = (bf16[256,1024]{1,0:T(8,128)(2,1)S(1)}, bf16[256,1024]{1,0:T(8,128)(2,1)}, u32[]{:S(2)}) copy-start(bf16[256,1024]{1,0:T(8,128)(2,1)} %param.7) | copy-start | bytes 1572868
  295.7 11.3 %copy-start.1 = (f32[256,5120]{1,0:T(8,128)S(1)}, f32[256,5120]{1,0:T(8,128)}, u32[]{:S(2)}) copy-start(f32[256,5120]{1,0:T(8,128)} %gather_fusion) | copy-start | bytes 15728644
Sparse Core Ops, SparseCore 0:
  9.6 286.1 all-gather.2
  297.3 43.5 all-gather.4
where the time goes:
time: 374 us; the launch traced here: 371 us
  waiting for transfers between devices  140 us (37%)
  blocking collectives  117 us (31%)
  local copies, waits for them, and re-layouts  43.9 us (12%)
  matrix products  27.6 us (7%)
  other arithmetic  19.4 us (5%)
  between operations  14.8 us (4%)
  starting transfers between devices  7.71 us (2%)
    all_to_all x1, blocking collectives, local(): lax.all_to_all(sliced, 'dp', split_axis=0, concat_axis=0, tiled=True)  108 us
    all_to_all x1, waiting for transfers between devices, local(): lax.all_to_all(pieces, ('dp', 'adapter'), split_axis=0, concat_axis=0, ti...  105 us
    all_gather x1, waiting for transfers between devices, local(): everyone = lax.all_gather(received, 'adapter', axis=0, tiled=True)  31.6 us
    scatter-add x1, other arithmetic, local(): adapter_grad = jnp.zeros((plugins_held_count, plugin_inner_dimension, mat...  16.4 us
    dot_general x1, matrix products, local(): jnp.einsum('tk,dk->td', loss_sensitivity, lax.all_gather(fixed_projection...  11.3 us
    gather x1, local copies, waits for them, and re-layouts, local(): adapter_input_gradient.reshape(padded, model_width)[element_slot_position]  10.8 us
    reshape x1, local copies, waits for them, and re-layouts, local(): plugin_factor_matrices.reshape(plugins_held_count, plugin_inner_dimension...  9.2 us
    unnamed x1, blocking collectives  8.92 us
  transfers between devices with their start and end apart: 3, of which 3 were waited for; matrix products, arithmetic and copies ran while one was open for 18% of the time, Pallas kernels for 0%

commit v1 on v0

v1 whole, which is shorter than its diff:
```python
import functools

import jax
import jax.numpy as jnp
from jax import lax
from jax.experimental import pallas as pl
from jax.experimental.pallas import tpu as pltpu
from jax.sharding import PartitionSpec as P

BLK = 128

adapter_scale = 2.0
MESH = pl.DeviceIdType.MESH
VMEM_LIMIT = 48 * 1024 * 1024


def remote(src, dst, send, recv, **where):
    return pltpu.make_async_remote_copy(
        src_ref=src, dst_ref=dst, send_sem=send, recv_sem=recv, device_id=where, device_id_type=MESH
    )


def greet(peers):
    barrier = pltpu.get_barrier_semaphore()
    nd = lax.axis_size("dp")
    me = lax.axis_index("dp")

    @pl.loop(1, nd)
    def _(o):
        pl.semaphore_signal(barrier, inc=1, device_id={"dp": lax.rem(me + o, nd)}, device_id_type=MESH)

    for peer in peers:
        pl.semaphore_signal(barrier, inc=1, device_id=peer, device_id_type=MESH)
    pl.semaphore_wait(barrier, nd - 1 + len(peers))


def fetch_kernel(
    nb, ids, cat, weight, fetched, gathered, pieces, from_core, from_x,
    s1, r1, s2, r2, s3, r3, sz, rz, sx, rx, sy, ry, sc, rc, local_sem,
):
    nd = lax.axis_size("dp")
    me = lax.axis_index("dp")
    g = lax.axis_index("group")
    a = lax.axis_index("adapter")
    x, c = a // 2, a % 2
    core = x * 2 + (1 - c)
    other = (1 - x) * 2 + c
    held, rank, _ = cat.shape
    greet([{"adapter": core}, {"adapter": other}, {"group": 1 - g}])

    def w_z(o):
        return remote(weight.at[c, g, x], gathered.at[me, c, g, x], sz.at[o], rz.at[o], dp=lax.rem(me + o, nd))

    def w_x(o):
        s = lax.rem(me + nd - o, nd)
        return remote(gathered.at[s, c, g, x], gathered.at[s, c, g, x], sx.at[o], rx.at[o], adapter=other)

    def w_y(o):
        s = lax.rem(me + nd - o, nd)
        return remote(gathered.at[s, c, g], gathered.at[s, c, g], sy.at[o], ry.at[o], group=1 - g)

    def w_c(o):
        s = lax.rem(me + nd - o, nd)
        return remote(gathered.at[s, c], gathered.at[s, c], sc.at[o], rc.at[o], adapter=core)

    def f_core(o):
        d = lax.rem(me + o, nd)
        return remote(pieces.at[d, 1 - c], from_core.at[d], s1.at[o], r1.at[o], adapter=core)

    def f_x(o):
        d = lax.rem(me + o, nd)
        return remote(pieces.at[d, c, 1 - x], from_x.at[d], s2.at[o], r2.at[o], adapter=other)

    def f_z(o):
        d = lax.rem(me + o, nd)
        return remote(pieces.at[d, c, x], fetched.at[me], s3.at[o], r3.at[o], dp=d)

    @pl.loop(1, nd)
    def _(o):
        w_z(o).start()

    own = pltpu.make_async_copy(weight, gathered.at[me], local_sem.at[0])
    own.start()

    @pl.loop(0, nd)
    def _(i):
        o = lax.rem(i + 1, nd)
        d = lax.rem(me + o, nd)

        @pl.loop(0, 4)
        def _(q):
            xx, cc = q // 2, q % 2
            for k in range(nb):
                local_id = ids[(d * 4 + q) * nb + k] - a * held
                valid = (local_id >= 0) & (local_id < held)
                row = cat[jnp.clip(local_id, 0, held - 1)]
                pieces[d, cc, xx, k * rank : (k + 1) * rank, :] = jnp.where(valid, row, jnp.zeros_like(row))

        f_core(o).start()

    @pl.loop(0, nd)
    def _(i):
        o = lax.rem(i + 1, nd)
        d = lax.rem(me + o, nd)
        f_core(o).wait_recv()
        pieces[d, c] += from_core[d]
        f_x(o).start()

    def x_done(o):
        d = lax.rem(me + o, nd)
        f_x(o).wait_recv()
        pieces[d, c, x] += from_x[d]

    @pl.loop(1, nd)
    def _(o):
        x_done(o)
        f_z(o).start()
        w_z(o).wait_recv()
        w_x(o).start()

    x_done(0)
    mine = pltpu.make_async_copy(pieces.at[me, c, x], fetched.at[me], local_sem.at[1])
    mine.start()

    @pl.loop(1, nd)
    def _(o):
        w_x(o).wait_recv()
        w_y(o).start()

    @pl.loop(1, nd)
    def _(o):
        w_y(o).wait_recv()
        w_c(o).start()

    @pl.loop(1, nd)
    def _(o):
        f_z(o).wait()
        w_z(o).wait_send()
        w_x(o).wait_send()
        w_y(o).wait_send()
        w_c(o).wait()

    @pl.loop(0, nd)
    def _(o):
        f_core(o).wait_send()
        f_x(o).wait_send()

    own.wait()
    mine.wait()


def fetch(ids, catalog, weight, nd, nb):
    held, rank, width = catalog.shape
    rows, kv = weight.shape
    weight = weight.reshape(2, 2, 2, rows // 8, kv)
    dma = pltpu.SemaphoreType.DMA((nd,))
    return pl.pallas_call(
        functools.partial(fetch_kernel, nb),
        out_shape=(
            jax.ShapeDtypeStruct((nd, nb * rank, width), jnp.bfloat16),
            jax.ShapeDtypeStruct((nd, 2, 2, 2, rows // 8, kv), jnp.bfloat16),
        ),
        in_specs=[
            pl.BlockSpec(memory_space=pltpu.SMEM),
            pl.BlockSpec(memory_space=pltpu.VMEM),
            pl.BlockSpec(memory_space=pl.ANY),
        ],
        out_specs=(pl.BlockSpec(memory_space=pl.ANY), pl.BlockSpec(memory_space=pl.ANY)),
        scratch_shapes=[
            pltpu.VMEM((nd, 2, 2, nb * rank, width), jnp.bfloat16),
            pltpu.VMEM((nd, 2, nb * rank, width), jnp.bfloat16),
            pltpu.VMEM((nd, nb * rank, width), jnp.bfloat16),
        ]
        + [dma] * 14
        + [pltpu.SemaphoreType.DMA((2,))],
        compiler_params=pltpu.CompilerParams(
            collective_id=0, has_side_effects=True, vmem_limit_bytes=VMEM_LIMIT
        ),
    )(ids, catalog, weight)


def exchange_kernel(grads, out, sz, rz, sx, rx, sc, rc, local_sem):
    nd = lax.axis_size("dp")
    me = lax.axis_index("dp")
    a = lax.axis_index("adapter")
    x, c = a // 2, a % 2
    core = x * 2 + (1 - c)
    other = (1 - x) * 2 + c
    greet([{"adapter": core}, {"adapter": other}])

    def g_z(o):
        d = lax.rem(me + o, nd)
        return remote(grads.at[d], out.at[me, x, c], sz.at[o], rz.at[o], dp=d)

    def g_x(o):
        s = lax.rem(me + nd - o, nd)
        return remote(out.at[s, x, c], out.at[s, x, c], sx.at[o], rx.at[o], adapter=other)

    def g_c(o):
        s = lax.rem(me + nd - o, nd)
        return remote(out.at[s, :, c], out.at[s, :, c], sc.at[o], rc.at[o], adapter=core)

    @pl.loop(1, nd)
    def _(o):
        g_z(o).start()

    own = pltpu.make_async_copy(grads.at[me], out.at[me, x, c], local_sem)
    own.start()
    own.wait()
    g_x(0).start()

    @pl.loop(1, nd)
    def _(o):
        g_z(o).wait_recv()
        g_x(o).start()

    @pl.loop(0, nd)
    def _(o):
        g_x(o).wait_recv()
        g_c(o).start()

    @pl.loop(1, nd)
    def _(o):
        g_z(o).wait_send()

    @pl.loop(0, nd)
    def _(o):
        g_x(o).wait_send()
        g_c(o).wait()


def exchange(grads):
    nd, rows, width = grads.shape
    dma = pltpu.SemaphoreType.DMA((nd,))
    return pl.pallas_call(
        exchange_kernel,
        out_shape=jax.ShapeDtypeStruct((nd, 2, 2, rows, width), jnp.bfloat16),
        in_specs=[pl.BlockSpec(memory_space=pl.ANY)],
        out_specs=pl.BlockSpec(memory_space=pl.ANY),
        scratch_shapes=[dma] * 6 + [pltpu.SemaphoreType.DMA],
        compiler_params=pltpu.CompilerParams(
            collective_id=1, has_side_effects=True, vmem_limit_bytes=VMEM_LIMIT
        ),
    )(grads)


def place_kernel(ids, rows, out):
    count = out.shape[0]
    base = pl.program_id(0) * count
    out[...] = jnp.zeros_like(out)

    @pl.loop(0, rows.shape[0])
    def _(s):
        target = ids[s] - base

        @pl.when((target >= 0) & (target < count))
        def _():
            out[target] += rows[s].astype(jnp.float32)


def place(ids, rows, held):
    total, rank, width = rows.shape
    step = 16
    return pl.pallas_call(
        place_kernel,
        out_shape=jax.ShapeDtypeStruct((held, rank, width), jnp.float32),
        grid_spec=pltpu.PrefetchScalarGridSpec(
            num_scalar_prefetch=1,
            grid=(held // step,),
            in_specs=[pl.BlockSpec((total, rank, width), lambda i, ids: (0, 0, 0))],
            out_specs=pl.BlockSpec((step, rank, width), lambda i, ids: (i, 0, 0)),
        ),
        compiler_params=pltpu.CompilerParams(vmem_limit_bytes=VMEM_LIMIT),
    )(ids, rows)


def local(
    layer_activation_matrix,
    loss_sensitivity,
    fixed_projection_matrix,
    plugin_factor_matrices,
    element_slot_position,
    segment_plugin_choice,
):
    token_count, model_width = layer_activation_matrix.shape
    block_count = segment_plugin_choice.shape[0]
    held, rank, width = plugin_factor_matrices.shape
    nd = lax.axis_size("dp")
    owner_index = lax.axis_index("adapter")
    ids = lax.all_gather(segment_plugin_choice, ("dp", "adapter"), axis=0, tiled=True)
    fetched, weight = fetch(ids, plugin_factor_matrices, fixed_projection_matrix, nd, block_count)
    weight = weight.reshape(model_width, loss_sensitivity.shape[1])
    columns = block_count * rank
    factors = jnp.transpose(fetched, (1, 0, 2)).reshape(columns, nd * width)
    down, up = factors[:, :model_width], factors[:, model_width:]
    owned = (element_slot_position // BLK)[:, None] == (jnp.arange(columns) // rank)[None, :]

    def dot(lhs, rhs, left, right):
        return lax.dot_general(
            lhs, rhs, (((left,), (right,)), ((), ())), preferred_element_type=jnp.float32
        )

    low_in = jnp.where(owned, dot(layer_activation_matrix, down, 1, 1).astype(jnp.bfloat16), 0)
    low_out = jnp.where(owned, dot(loss_sensitivity, up, 1, 1).astype(jnp.bfloat16), 0)
    down_grad = (adapter_scale * dot(low_out, layer_activation_matrix, 0, 0)).astype(jnp.bfloat16)
    up_grad = (adapter_scale * dot(low_in, loss_sensitivity, 0, 0)).astype(jnp.bfloat16)
    grads = jnp.concatenate([down_grad, up_grad], axis=1).reshape(columns, nd, width)
    everyone = exchange(jnp.transpose(grads, (1, 0, 2)))
    adapter_grad = place(
        ids - owner_index * held, everyone.reshape(ids.shape[0], rank, width), held
    )
    frozen = dot(loss_sensitivity, weight, 1, 1).astype(jnp.bfloat16)
    frozen = lax.optimization_barrier(frozen).astype(jnp.float32)
    input_token_gradient = (frozen + adapter_scale * dot(low_out, down, 1, 0)).astype(jnp.bfloat16)
    return (input_token_gradient, adapter_grad)


def solution(mesh):
    return jax.shard_map(
        local,
        mesh=mesh,
        in_specs=(
            P(("group", "dp", "adapter"), None),
            P(("group", "dp", "adapter"), None),
            P("dp", None),
            P("adapter", None, "dp"),
            P(("group", "dp", "adapter")),
            P(("group", "dp", "adapter")),
        ),
        out_specs=(P(("group", "dp", "adapter"), None), P(("group", "adapter"), None, "dp")),
        check_vma=False,
    )
```

time: 374 us -> 167 us (0.45)
  the two profiles are of different devices: /device:TPU:3 before, /device:TPU:25 now
where the time goes in v1:
time: 167 us
  Pallas kernels  136 us (81%)
  matrix products  12.5 us (7%)
  local copies, waits for them, and re-layouts  9.1 us (5%)
  blocking collectives  6.46 us (4%)
    pallas_call x1, Pallas kernels, fetch(): pl.pallas_call(functools.partial(fetch_kernel, nb), out_shape=(jax.ShapeD...  86.1 us
    pallas_call x1, Pallas kernels, exchange(): pl.pallas_call(exchange_kernel, out_shape=jax.ShapeDtypeStruct((nd, 2, 2,...  39.7 us
    dot_general x5, matrix products, dot(): lax.dot_general(lhs, rhs, (((left,), (right,)), ((), ())), preferred_elem...  12.5 us
    pallas_call x1, Pallas kernels, place(): pl.pallas_call(place_kernel, out_shape=jax.ShapeDtypeStruct((held, rank,...  10.6 us
    unnamed x14, local copies, waits for them, and re-layouts  8.99 us
    unnamed x1, blocking collectives  6.46 us

profile of v1, /device:TPU:25, one launch (start us, length us, event | category | flops | bytes accessed | tf_op | source)
XLA Modules:
  0.0 166.6 jit_solution(729555787677412727)
XLA Ops:
  0.6 0.0 copy-start
  0.6 1.4 dynamic-slice
  2.7 0.9 dynamic-update-slice
  3.6 6.5 %all-reduce.ids = s32[64]{0:T(128)S(1)} all-reduce(s32[64]{0:T(128)S(1)} %dynamic-update-slice), channel_id=1, replica_groups=mesh['group'=2,'dp'=4,'adapter'=4] {'dp','adapter'}, use_global_device_ids=true, to_apply=%add | all-reduce | flops 64 | bytes 512
  10.0 0.7 and_select_fusion.1
  10.7 0.0 copy-start.1
  10.7 1.7 %copy-done.1 = bf16[1280,1024]{1,0:T(8,128)(2,1)S(1)} copy-done((bf16[1280,1024]{1,0:T(8,128)(2,1)S(1)}, bf16[1280,1024]{1,0:T(8,128)(2,1)}, u32[]{:S(2)}) %copy-start.1) | copy-done | bytes 2621464
  12.5 0.0 copy-start.2
  12.5 86.1 %shard_map.77 = (bf16[4,64,1536]{2,1,0:T(8,128)(2,1)S(1)}, bf16[4,2,2,2,160,1024]{5,4,3,2,1,0:T(8,128)(2,1)}) custom-call(s32[64]{0:T(128)S(1)} %all-reduce.ids, bf16[128,16,1536]{2,1,0:T(8,128)(2,1)} %cat.1, bf16[2,2,2,160,1024]{4,3,2,1,0:T(8,128)(2,1)S(1)} %bitcast.36), custom_call_target="tpu_custom_call" | custom-call | tf_op jit(solution)/shard_map/pallas_call | solution.py:157
  98.5 0.0 copy-done.2
  98.6 6.9 %fusion.2 = bf16[256,5120]{0,1:T(8,128)(2,1)S(1)} fusion(bf16[5120,1024]{1,0:T(8,128)(2,1)} %bitcast.42, bf16[256,1024]{1,0:T(8,128)(2,1)S(1)} %copy-done.2), kind=kOutput, calls=%fused_computation.4 | convolution fusion | flops 2685665280 | bytes 13631488 | tf_op jit(solution)/shard_map/dot_general | solution.py:299
  105.5 0.1 copy.16
  105.5 0.3 fusion.6
  105.8 0.0 copy-start.3
  105.8 0.6 copy-done.3
  106.4 2.5 %fusion.1 = bf16[256,5120]{0,1:T(8,128)(2,1)} fusion(bf16[256,64]{0,1:T(8,128)(2,1)S(1)} %fusion.6, bf16[256,5120]{0,1:T(8,128)(2,1)S(1)} %fusion.2, bf16[64,6144]{1,0:T(8,128)(2,1)S(1)} %bitcast.39), kind=kOutput, calls=%fused_computation.2 | convolution fusion | flops 173015040 | bytes 5931008 | tf_op jit(solution)/shard_map/dot_general | solution.py:299
  108.9 0.0 copy-done
  108.9 2.2 %fusion.4 = bf16[64,1024]{1,0:T(8,128)(2,1)S(1)} fusion(bf16[256,1024]{1,0:T(8,128)(2,1)} %param.7, bf16[256,5120]{1,0:T(8,128)(2,1)S(1)} %copy-done, bf16[64,6144]{1,0:T(8,128)(2,1)S(1)} %bitcast.40, s32[256]{0:T(256)S(1)} %and_select_fusion.1, s32[64]{0:T(128)S(1)} %and_select_fusion), kind=kOutput, calls=%fused_computation.8 | convolution fusion | flops 201506816 | bytes 3933696 | tf_op jit(solution)/shard_map/dot_general | solution.py:299
  111.2 0.0 copy-start.4
  111.2 4.4 %copy.13 = bf16[256,5120]{1,0:T(8,128)(2,1)} copy(bf16[256,5120]{0,1:T(8,128)(2,1)} %fusion.1) | data formatting | bytes 5242880
  115.5 0.0 copy-done.4
  115.5 0.6 fusion.3
  116.1 0.1 pad_maximum_fusion
  116.2 0.1 copy.18
  116.2 39.7 %shard_map.78 = bf16[4,2,2,64,1536]{4,3,2,1,0:T(8,128)(2,1)S(1)} custom-call(bf16[4,64,1536]{2,1,0:T(8,128)(2,1)S(1)} %bitcast.35), custom_call_target="tpu_custom_call" | custom-call | tf_op jit(solution)/shard_map/pallas_call | solution.py:235
  156.0 10.6 %shard_map.79 = f32[128,16,1536]{2,1,0:T(8,128)} custom-call(s32[64]{0:T(128)S(1)} %broadcast_subtract_fusion.ids, bf16[64,16,1536]{2,1,0:T(8,128)(2,1)S(1)} %bitcast.34), custom_call_target="tpu_custom_call" | custom-call | tf_op jit(solution)/shard_map/pallas_call | solution.py:264
  (3 shorter events, 0.0 us)
Async XLA Ops:
  0.6 108.3 %copy-start = (bf16[256,5120]{1,0:T(8,128)(2,1)S(1)}, bf16[256,5120]{1,0:T(8,128)(2,1)}, u32[]{:S(2)}) copy-start(bf16[256,5120]{1,0:T(8,128)(2,1)} %param.6) | copy-start | bytes 7864324
  10.7 1.7 %copy-start.1 = (bf16[1280,1024]{1,0:T(8,128)(2,1)S(1)}, bf16[1280,1024]{1,0:T(8,128)(2,1)}, u32[]{:S(2)}) copy-start(bf16[1280,1024]{1,0:T(8,128)(2,1)} %param.8) | copy-start | bytes 7864324
  12.5 86.1 %copy-start.2 = (bf16[256,1024]{1,0:T(8,128)(2,1)S(1)}, bf16[256,1024]{1,0:T(8,128)(2,1)}, u32[]{:S(2)}) copy-start(bf16[256,1024]{1,0:T(8,128)(2,1)} %param.7) | copy-start | bytes 1572868
  105.8 0.6 copy-start.3
  111.2 4.4 %copy-start.4 = (bf16[256,64]{0,1:T(8,128)(2,1)S(1)}, bf16[256,64]{0,1:T(8,128)(2,1)}, u32[]{:S(2)}) copy-start(bf16[256,64]{0,1:T(8,128)(2,1)} %copy-done.3) | copy-start | bytes 98308

commit v2 on v1

--- a/solution.py
+++ b/solution.py
@@ -244,6 +244,241 @@
     )(grads)
 
 
+def whole_kernel(
+    nb, ids, cat, weight, tokens, cotangent, owned, gradient, out,
+    pieces, from_core, from_x, fetched, gathered, frozen, factors, grads,
+    s1, r1, s2, r2, s3, r3, sz, rz, sx, rx, sy, ry, sc, rc, gsz, grz, gsx, grx, gsc, grc, local_sem,
+):
+    nd = lax.axis_size("dp")
+    me = lax.axis_index("dp")
+    g = lax.axis_index("group")
+    a = lax.axis_index("adapter")
+    x, c = a // 2, a % 2
+    core = x * 2 + (1 - c)
+    other = (1 - x) * 2 + c
+    held, rank, width = cat.shape
+    model_width = tokens.shape[1]
+    shard = model_width // nd
+    greet([{"adapter": core}, {"adapter": other}, {"group": 1 - g}])
+
+    def after(o):
+        return lax.rem(me + o, nd)
+
+    def before(o):
+        return lax.rem(me + nd - o, nd)
+
+    def w_z(o):
+        return remote(weight.at[c, g, x], gathered.at[me, c, g, x], sz.at[o], rz.at[o], dp=after(o))
+
+    def w_x(o):
+        block = gathered.at[before(o), c, g, x]
+        return remote(block, block, sx.at[o], rx.at[o], adapter=other)
+
+    def w_y(o):
+        block = gathered.at[before(o), c, g]
+        return remote(block, block, sy.at[o], ry.at[o], group=1 - g)
+
+    def w_c(o):
+        block = gathered.at[before(o), c]
+        return remote(block, block, sc.at[o], rc.at[o], adapter=core)
+
+    def f_core(o):
+        d = after(o)
+        return remote(pieces.at[d, 1 - c], from_core.at[d], s1.at[o], r1.at[o], adapter=core)
+
+    def f_x(o):
+        d = after(o)
+        return remote(pieces.at[d, c, 1 - x], from_x.at[d], s2.at[o], r2.at[o], adapter=other)
+
+    def f_z(o):
+        d = after(o)
+        return remote(pieces.at[d, c, x], fetched.at[me], s3.at[o], r3.at[o], dp=d)
+
+    def g_z(o):
+        d = after(o)
+        return remote(grads.at[d], out.at[me, x, c], gsz.at[o], grz.at[o], dp=d)
+
+    def g_x(o):
+        block = out.at[before(o), x, c]
+        return remote(block, block, gsx.at[o], grx.at[o], adapter=other)
+
+    def g_c(o):
+        block = out.at[before(o), :, c]
+        return remote(block, block, gsc.at[o], grc.at[o], adapter=core)
+
+    def dot(lhs, rhs, left, right):
+        return lax.dot_general(
+            lhs, rhs, (((left,), (right,)), ((), ())), preferred_element_type=jnp.float32
+        )
+
+    def freeze(s):
+        rows = gathered[s].reshape(shard, gathered.shape[-1])
+        frozen[s] = dot(cotangent[...], rows, 1, 1).astype(jnp.bfloat16)
+
+    @pl.loop(1, nd)
+    def _(o):
+        w_z(o).start()
+
+    own = pltpu.make_async_copy(weight, gathered.at[me], local_sem.at[0])
+    own.start()
+
+    @pl.loop(0, nd)
+    def _(i):
+        o = lax.rem(i + 1, nd)
+        d = after(o)
+
+        @pl.loop(0, 4)
+        def _(q):
+            xx, cc = q // 2, q % 2
+            for k in range(nb):
+                local_id = ids[(d * 4 + q) * nb + k] - a * held
+                valid = (local_id >= 0) & (local_id < held)
+                row = cat[jnp.clip(local_id, 0, held - 1)]
+                pieces[d, cc, xx, k * rank : (k + 1) * rank, :] = jnp.where(valid, row, jnp.zeros_like(row))
+
+        f_core(o).start()
+
+    @pl.loop(0, nd)
+    def _(i):
+        o = lax.rem(i + 1, nd)
+        d = after(o)
+        f_core(o).wait_recv()
+        pieces[d, c] += from_core[d]
+        f_x(o).start()
+
+    def x_done(o):
+        d = after(o)
+        f_x(o).wait_recv()
+        pieces[d, c, x] += from_x[d]
+
+    @pl.loop(1, nd)
+    def _(o):
+        x_done(o)
+        f_z(o).start()
+        w_z(o).wait_recv()
+        w_x(o).start()
+
+    x_done(0)
+    fetched[me] = pieces[me, c, x]
+    own.wait()
+    freeze(me)
+    w_x(1).wait_recv()
+    w_y(1).start()
+
+    @pl.loop(1, nd)
+    def _(o):
+        f_z(o).wait_recv()
+
+    for j in range(nd):
+        factors[:, j * width : (j + 1) * width] = fetched[j]
+    mask = owned[...] > 0
+    low_out = dot(cotangent[...], factors[:, model_width:], 1, 1)
+    low_out = jnp.where(mask, low_out, 0.0).astype(jnp.bfloat16)
+    low_in = dot(tokens[...], factors[:, :model_width], 1, 1)
+    low_in = jnp.where(mask, low_in, 0.0).astype(jnp.bfloat16)
+    for j in range(nd):
+        inner = min(max(model_width - j * width, 0), width)
+        if inner:
+            part = dot(low_out, tokens[:, j * width : j * width + inner], 0, 0)
+            grads[j, :, :inner] = (adapter_scale * part).astype(jnp.bfloat16)
+        if inner < width:
+            start = j * width + inner - model_width
+            part = dot(low_in, cotangent[:, start : start + width - inner], 0, 0)
+            grads[j, :, inner:] = (adapter_scale * part).astype(jnp.bfloat16)
+
+    @pl.loop(1, nd)
+    def _(o):
+        g_z(o).start()
+
+    mine = pltpu.make_async_copy(grads.at[me], out.at[me, x, c], local_sem.at[1])
+    mine.start()
+    mine.wait()
+    g_x(0).start()
+
+    @pl.loop(2, nd)
+    def _(o):
+        w_x(o).wait_recv()
+        w_y(o).start()
+
+    @pl.loop(1, nd)
+    def _(o):
+        g_z(o).wait_recv()
+        g_x(o).start()
+
+    w_y(1).wait_recv()
+    w_c(1).start()
+
+    @pl.loop(0, nd)
+    def _(o):
+        g_x(o).wait_recv()
+        g_c(o).start()
+
+    @pl.loop(2, nd)
+    def _(o):
+        w_y(o).wait_recv()
+        w_c(o).start()
+
+    @pl.loop(1, nd)
+    def _(o):
+        w_c(o).wait_recv()
+        freeze(before(o))
+
+    for s in range(nd):
+        columns = slice(s * shard, (s + 1) * shard)
+        extra = dot(low_out, factors[:, columns], 1, 0)
+        gradient[:, columns] = (frozen[s].astype(jnp.float32) + adapter_scale * extra).astype(jnp.bfloat16)
+
+    @pl.loop(1, nd)
+    def _(o):
+        f_z(o).wait_send()
+        w_z(o).wait_send()
+        w_x(o).wait_send()
+        w_y(o).wait_send()
+        w_c(o).wait_send()
+        g_z(o).wait_send()
+
+    @pl.loop(0, nd)
+    def _(o):
+        f_core(o).wait_send()
+        f_x(o).wait_send()
+        g_x(o).wait_send()
+        g_c(o).wait()
+
+
+def whole(ids, catalog, weight, tokens, cotangent, owned, nd, nb):
+    held, rank, width = catalog.shape
+    rows, kv = weight.shape
+    columns = nb * rank
+    weight = weight.reshape(2, 2, 2, rows // 8, kv)
+    dma = pltpu.SemaphoreType.DMA((nd,))
+    vmem = pl.BlockSpec(memory_space=pltpu.VMEM)
+    anywhere = pl.BlockSpec(memory_space=pl.ANY)
+    return pl.pallas_call(
+        functools.partial(whole_kernel, nb),
+        out_shape=(
+            jax.ShapeDtypeStruct(tokens.shape, jnp.bfloat16),
+            jax.ShapeDtypeStruct((nd, 2, 2, columns, width), jnp.bfloat16),
+        ),
+        in_specs=[pl.BlockSpec(memory_space=pltpu.SMEM), vmem, anywhere, vmem, vmem, vmem],
+        out_specs=(vmem, anywhere),
+        scratch_shapes=[
+            pltpu.VMEM((nd, 2, 2, columns, width), jnp.bfloat16),
+            pltpu.VMEM((nd, 2, columns, width), jnp.bfloat16),
+            pltpu.VMEM((nd, columns, width), jnp.bfloat16),
+            pltpu.VMEM((nd, columns, width), jnp.bfloat16),
+            pltpu.VMEM((nd, 2, 2, 2, rows // 8, kv), jnp.bfloat16),
+            pltpu.VMEM((nd, tokens.shape[0], rows), jnp.bfloat16),
+            pltpu.VMEM((columns, nd * width), jnp.bfloat16),
+            pltpu.VMEM((nd, columns, width), jnp.bfloat16),
+        ]
+        + [dma] * 20
+        + [pltpu.SemaphoreType.DMA((2,))],
+        compiler_params=pltpu.CompilerParams(
+            collective_id=2, has_side_effects=True, vmem_limit_bytes=VMEM_LIMIT
+        ),
+    )(ids, catalog, weight, tokens, cotangent, owned)
+
+
 def place_kernel(ids, rows, out):
     count = out.shape[0]
     base = pl.program_id(0) * count
@@ -288,12 +523,25 @@
     nd = lax.axis_size("dp")
     owner_index = lax.axis_index("adapter")
     ids = lax.all_gather(segment_plugin_choice, ("dp", "adapter"), axis=0, tiled=True)
+    columns = block_count * rank
+    owned = (element_slot_position // BLK)[:, None] == (jnp.arange(columns) // rank)[None, :]
+    if width % 128 == 0 and model_width // nd % 128 == 0:
+        input_token_gradient, everyone = whole(
+            ids,
+            plugin_factor_matrices,
+            fixed_projection_matrix,
+            layer_activation_matrix,
+            loss_sensitivity,
+            owned.astype(jnp.float32),
+            nd,
+            block_count,
+        )
+        everyone = everyone.reshape(ids.shape[0], rank, width)
+        return (input_token_gradient, place(ids - owner_index * held, everyone, held))
     fetched, weight = fetch(ids, plugin_factor_matrices, fixed_projection_matrix, nd, block_count)
     weight = weight.reshape(model_width, loss_sensitivity.shape[1])
-    columns = block_count * rank
     factors = jnp.transpose(fetched, (1, 0, 2)).reshape(columns, nd * width)
     down, up = factors[:, :model_width], factors[:, model_width:]
-    owned = (element_slot_position // BLK)[:, None] == (jnp.arange(columns) // rank)[None, :]
 
     def dot(lhs, rhs, left, right):
         return lax.dot_general(

time: 167 us -> 126 us (0.75)
  the two profiles are of different devices: /device:TPU:25 before, /device:TPU:9 now
where the time goes in v2:
time: 126 us; the launch traced here: 125 us
  Pallas kernels  106 us (84%)
  blocking collectives  8.71 us (7%)
  local copies, waits for them, and re-layouts  8.25 us (7%)
  between operations  1.33 us (1%)
    pallas_call x1, Pallas kernels, whole(): pl.pallas_call(functools.partial(whole_kernel, nb), out_shape=(jax.ShapeD...  95.6 us
    pallas_call x1, Pallas kernels, place(): pl.pallas_call(place_kernel, out_shape=jax.ShapeDtypeStruct((held, rank,...  10.7 us
    unnamed x1, blocking collectives  8.71 us
    unnamed x10, local copies, waits for them, and re-layouts  8.25 us

profile of v2, /device:TPU:9, one launch (start us, length us, event | category | flops | bytes accessed | tf_op | source)
XLA Modules:
  0.0 125.4 jit_solution(17597641376448341436)
XLA Ops:
  0.6 1.2 dynamic-slice
  2.5 0.9 dynamic-update-slice
  3.4 8.7 %all-reduce.ids = s32[64]{0:T(128)S(1)} all-reduce(s32[64]{0:T(128)S(1)} %dynamic-update-slice), channel_id=1, replica_groups=mesh['group'=2,'dp'=4,'adapter'=4] {'dp','adapter'}, use_global_device_ids=true, to_apply=%add | all-reduce | flops 64 | bytes 512
  12.1 0.7 and_select_fusion.1
  12.8 0.1 compare_convert_fusion.owned
  12.9 0.0 copy-start.1
  12.9 1.7 %copy-done.1 = bf16[1280,1024]{1,0:T(8,128)(2,1)S(1)} copy-done((bf16[1280,1024]{1,0:T(8,128)(2,1)S(1)}, bf16[1280,1024]{1,0:T(8,128)(2,1)}, u32[]{:S(2)}) %copy-start.1) | copy-done | bytes 2621464
  14.7 0.0 copy-start.2
  14.7 1.0 copy-done.2
  15.7 95.6 %shard_map.77 = (bf16[256,5120]{1,0:T(8,128)(2,1)S(1)}, bf16[4,2,2,64,1536]{4,3,2,1,0:T(8,128)(2,1)}) custom-call(s32[64]{0:T(128)S(1)} %all-reduce.ids, bf16[128,16,1536]{2,1,0:T(8,128)(2,1)} %cat.1, bf16[2,2,2,160,1024]{4,3,2,1,0:T(8,128)(2,1)S(1)} %bitcast.4, bf16[256,5120]{1,0:T(8,128)(2,1)} %tokens.1, bf16[256,1024]{1,0:T(8,128)(2,1)S(1)} %copy-done.2, ...), custom_call_target="tpu_custom_call" | custom-call | tf_op jit(solution)/shard_map/pallas_call | solution.py:456
  111.3 0.0 copy-start
  111.3 1.9 %copy-done = bf16[4,2,2,64,1536]{4,3,2,1,0:T(8,128)(2,1)S(1)} copy-done((bf16[4,2,2,64,1536]{4,3,2,1,0:T(8,128)(2,1)S(1)}, bf16[4,2,2,64,1536]{4,3,2,1,0:T(8,128)(2,1)}, u32[]{:S(2)}) %copy-start) | copy-done | bytes 3145752
  113.2 10.7 %shard_map.78 = f32[128,16,1536]{2,1,0:T(8,128)} custom-call(s32[64]{0:T(128)S(1)} %broadcast_subtract_fusion.ids, bf16[64,16,1536]{2,1,0:T(8,128)(2,1)S(1)} %bitcast.3), custom_call_target="tpu_custom_call" | custom-call | tf_op jit(solution)/shard_map/pallas_call | solution.py:499
  123.9 1.5 %copy.10 = bf16[256,5120]{1,0:T(8,128)(2,1)} copy(bf16[256,5120]{1,0:T(8,128)(2,1)S(1)} %get-tuple-element.8) | data formatting | bytes 5242880
  (3 shorter events, 0.0 us)
Async XLA Ops:
  12.9 1.7 %copy-start.1 = (bf16[1280,1024]{1,0:T(8,128)(2,1)S(1)}, bf16[1280,1024]{1,0:T(8,128)(2,1)}, u32[]{:S(2)}) copy-start(bf16[1280,1024]{1,0:T(8,128)(2,1)} %param.8) | copy-start | bytes 7864324
  14.7 1.0 copy-start.2
  111.3 1.9 %copy-start = (bf16[4,2,2,64,1536]{4,3,2,1,0:T(8,128)(2,1)S(1)}, bf16[4,2,2,64,1536]{4,3,2,1,0:T(8,128)(2,1)}, u32[]{:S(2)}) copy-start(bf16[4,2,2,64,1536]{4,3,2,1,0:T(8,128)(2,1)} %get-tuple-element.5) | copy-start | bytes 9437188

commit v3 on v2

--- a/solution.py
+++ b/solution.py
@@ -245,9 +245,9 @@
 
 
 def whole_kernel(
-    nb, ids, cat, weight, tokens, cotangent, owned, gradient, out,
-    pieces, from_core, from_x, fetched, gathered, frozen, factors, grads,
-    s1, r1, s2, r2, s3, r3, sz, rz, sx, rx, sy, ry, sc, rc, gsz, grz, gsx, grx, gsc, grc, local_sem,
+    nb, choice, cat_in, weight, tokens_in, cotangent, owned, gradient, out, spread,
+    cat, tokens, ids, pieces, from_core, from_x, fetched, gathered, frozen, factors, grads,
+    s1, r1, s2, r2, s3, r3, sz, rz, sx, rx, sy, ry, sc, rc, gsz, grz, gsx, grx, gsc, grc, ssa, rsa, ssb, rsb, local_sem,
 ):
     nd = lax.axis_size("dp")
     me = lax.axis_index("dp")
@@ -259,7 +259,8 @@
     held, rank, width = cat.shape
     model_width = tokens.shape[1]
     shard = model_width // nd
-    greet([{"adapter": core}, {"adapter": other}, {"group": 1 - g}])
+    across = (1 - x) * 2 + (1 - c)
+    greet([{"adapter": core}, {"adapter": other}, {"adapter": across}, {"group": 1 - g}])
 
     def after(o):
         return lax.rem(me + o, nd)
@@ -305,6 +306,13 @@
     def g_c(o):
         block = out.at[before(o), :, c]
         return remote(block, block, gsc.at[o], grc.at[o], adapter=core)
+
+    def i_z(o):
+        return remote(choice, spread.at[me, a], ssa.at[o], rsa.at[o], dp=after(o))
+
+    def i_a(k):
+        block = spread.at[:, a]
+        return remote(block, block, ssb.at[k], rsb.at[k], adapter=lax.rem(a + k, 4))
 
     def dot(lhs, rhs, left, right):
         return lax.dot_general(
@@ -317,10 +325,38 @@
 
     @pl.loop(1, nd)
     def _(o):
+        i_z(o).start()
+
+    @pl.loop(1, nd)
+    def _(o):
         w_z(o).start()
+
+    load_cat = pltpu.make_async_copy(cat_in, cat, local_sem.at[2])
+    load_cat.start()
+    load_tokens = pltpu.make_async_copy(tokens_in, tokens, local_sem.at[3])
+    load_tokens.start()
+    spread[me, a] = choice[...]
 
     own = pltpu.make_async_copy(weight, gathered.at[me], local_sem.at[0])
     own.start()
+
+    @pl.loop(1, nd)
+    def _(o):
+        i_z(o).wait_recv()
+
+    @pl.loop(1, 4)
+    def _(k):
+        i_a(k).start()
+
+    load_cat.wait()
+
+    @pl.loop(1, 4)
+    def _(k):
+        i_a(k).wait_recv()
+
+    to_scalar = pltpu.make_async_copy(spread, ids, local_sem.at[4])
+    to_scalar.start()
+    to_scalar.wait()
 
     @pl.loop(0, nd)
     def _(i):
@@ -331,7 +367,7 @@
         def _(q):
             xx, cc = q // 2, q % 2
             for k in range(nb):
-                local_id = ids[(d * 4 + q) * nb + k] - a * held
+                local_id = ids[d, q, 0, k] - a * held
                 valid = (local_id >= 0) & (local_id < held)
                 row = cat[jnp.clip(local_id, 0, held - 1)]
                 pieces[d, cc, xx, k * rank : (k + 1) * rank, :] = jnp.where(valid, row, jnp.zeros_like(row))
@@ -371,6 +407,7 @@
 
     for j in range(nd):
         factors[:, j * width : (j + 1) * width] = fetched[j]
+    load_tokens.wait()
     mask = owned[...] > 0
     low_out = dot(cotangent[...], factors[:, model_width:], 1, 1)
     low_out = jnp.where(mask, low_out, 0.0).astype(jnp.bfloat16)
@@ -430,6 +467,7 @@
 
     @pl.loop(1, nd)
     def _(o):
+        i_z(o).wait_send()
         f_z(o).wait_send()
         w_z(o).wait_send()
         w_x(o).wait_send()
@@ -444,8 +482,12 @@
         g_x(o).wait_send()
         g_c(o).wait()
 
-
-def whole(ids, catalog, weight, tokens, cotangent, owned, nd, nb):
+    @pl.loop(1, 4)
+    def _(k):
+        i_a(k).wait_send()
+
+
+def whole(choice, catalog, weight, tokens, cotangent, owned, nd, nb):
     held, rank, width = catalog.shape
     rows, kv = weight.shape
     columns = nb * rank
@@ -458,10 +500,14 @@
         out_shape=(
             jax.ShapeDtypeStruct(tokens.shape, jnp.bfloat16),
             jax.ShapeDtypeStruct((nd, 2, 2, columns, width), jnp.bfloat16),
+            jax.ShapeDtypeStruct((nd, 4) + choice.shape, jnp.int32),
         ),
-        in_specs=[pl.BlockSpec(memory_space=pltpu.SMEM), vmem, anywhere, vmem, vmem, vmem],
-        out_specs=(vmem, anywhere),
+        in_specs=[vmem, anywhere, anywhere, anywhere, vmem, vmem],
+        out_specs=(vmem, anywhere, vmem),
         scratch_shapes=[
+            pltpu.VMEM(catalog.shape, jnp.bfloat16),
+            pltpu.VMEM(tokens.shape, jnp.bfloat16),
+            pltpu.SMEM((nd, 4) + choice.shape, jnp.int32),
             pltpu.VMEM((nd, 2, 2, columns, width), jnp.bfloat16),
             pltpu.VMEM((nd, 2, columns, width), jnp.bfloat16),
             pltpu.VMEM((nd, columns, width), jnp.bfloat16),
@@ -471,39 +517,67 @@
             pltpu.VMEM((columns, nd * width), jnp.bfloat16),
             pltpu.VMEM((nd, columns, width), jnp.bfloat16),
         ]
-        + [dma] * 20
-        + [pltpu.SemaphoreType.DMA((2,))],
+        + [dma] * 22 + [pltpu.SemaphoreType.DMA((4,))] * 2
+        + [pltpu.SemaphoreType.DMA((5,))],
         compiler_params=pltpu.CompilerParams(
             collective_id=2, has_side_effects=True, vmem_limit_bytes=VMEM_LIMIT
         ),
-    )(ids, catalog, weight, tokens, cotangent, owned)
-
-
-def place_kernel(ids, rows, out):
-    count = out.shape[0]
-    base = pl.program_id(0) * count
-    out[...] = jnp.zeros_like(out)
-
-    @pl.loop(0, rows.shape[0])
-    def _(s):
-        target = ids[s] - base
-
-        @pl.when((target >= 0) & (target < count))
+    )(choice, catalog, weight, tokens, cotangent, owned)
+
+
+def place_kernel(nb, ids, rows, out, head, following):
+    count, rank, width = out.shape
+    step = pl.program_id(0)
+    held = count * pl.num_programs(0)
+    base = lax.axis_index("adapter") * held
+
+    @pl.when(step == 0)
+    def _():
+        @pl.loop(0, held, unroll=8)
+        def _(i):
+            head[i] = -1
+
+        @pl.loop(0, ids.shape[0])
+        def _(device):
+            for k in range(nb):
+                target = ids[device, k] - base
+
+                @pl.when((target >= 0) & (target < held))
+                def _():
+                    following[device * nb + k] = head[target]
+                    head[target] = device * nb + k
+
+    @pl.loop(0, count)
+    def _(i):
+        first = head[step * count + i]
+
+        @pl.when(first < 0)
         def _():
-            out[target] += rows[s].astype(jnp.float32)
-
-
-def place(ids, rows, held):
+            out[i] = jnp.zeros((rank, width), jnp.float32)
+
+        @pl.when(first >= 0)
+        def _():
+            out[i] = rows[first].astype(jnp.float32)
+
+            def add(s):
+                out[i] += rows[s].astype(jnp.float32)
+                return following[s]
+
+            lax.while_loop(lambda s: s >= 0, add, following[first])
+
+
+def place(ids, rows, held, nb):
     total, rank, width = rows.shape
     step = 16
     return pl.pallas_call(
-        place_kernel,
+        functools.partial(place_kernel, nb),
         out_shape=jax.ShapeDtypeStruct((held, rank, width), jnp.float32),
         grid_spec=pltpu.PrefetchScalarGridSpec(
             num_scalar_prefetch=1,
             grid=(held // step,),
             in_specs=[pl.BlockSpec((total, rank, width), lambda i, ids: (0, 0, 0))],
             out_specs=pl.BlockSpec((step, rank, width), lambda i, ids: (i, 0, 0)),
+            scratch_shapes=[pltpu.SMEM((held,), jnp.int32), pltpu.SMEM((total,), jnp.int32)],
         ),
         compiler_params=pltpu.CompilerParams(vmem_limit_bytes=VMEM_LIMIT),
     )(ids, rows)
@@ -521,13 +595,12 @@
     block_count = segment_plugin_choice.shape[0]
     held, rank, width = plugin_factor_matrices.shape
     nd = lax.axis_size("dp")
-    owner_index = lax.axis_index("adapter")
-    ids = lax.all_gather(segment_plugin_choice, ("dp", "adapter"), axis=0, tiled=True)
     columns = block_count * rank
     owned = (element_slot_position // BLK)[:, None] == (jnp.arange(columns) // rank)[None, :]
     if width % 128 == 0 and model_width // nd % 128 == 0:
-        input_token_gradient, everyone = whole(
-            ids,
+        choice = jnp.pad(segment_plugin_choice[None, :], ((0, 7), (0, 128 - block_count)))
+        input_token_gradient, everyone, spread = whole(
+            choice,
             plugin_factor_matrices,
             fixed_projection_matrix,
             layer_activation_matrix,
@@ -536,8 +609,10 @@
             nd,
             block_count,
         )
-        everyone = everyone.reshape(ids.shape[0], rank, width)
-        return (input_token_gradient, place(ids - owner_index * held, everyone, held))
+        ids = spread[:, :, 0, :].reshape(nd * 4, 128)
+        everyone = everyone.reshape(nd * 4 * block_count, rank, width)
+        return (input_token_gradient, place(ids, everyone, held, block_count))
+    ids = lax.all_gather(segment_plugin_choice, ("dp", "adapter"), axis=0, tiled=True)
     fetched, weight = fetch(ids, plugin_factor_matrices, fixed_projection_matrix, nd, block_count)
     weight = weight.reshape(model_width, loss_sensitivity.shape[1])
     factors = jnp.transpose(fetched, (1, 0, 2)).reshape(columns, nd * width)
@@ -555,7 +630,7 @@
     grads = jnp.concatenate([down_grad, up_grad], axis=1).reshape(columns, nd, width)
     everyone = exchange(jnp.transpose(grads, (1, 0, 2)))
     adapter_grad = place(
-        ids - owner_index * held, everyone.reshape(ids.shape[0], rank, width), held
+        ids.reshape(nd * 4, block_count), everyone.reshape(ids.shape[0], rank, width), held, block_count
     )
     frozen = dot(loss_sensitivity, weight, 1, 1).astype(jnp.bfloat16)
     frozen = lax.optimization_barrier(frozen).astype(jnp.float32)

time: 126 us -> 118 us (0.937)
  the two profiles are of different devices: /device:TPU:9 before, /device:TPU:3 now
where the time goes in v3:
time: 118 us; the launch traced here: 117 us
  Pallas kernels  109 us (92%)
  local copies, waits for them, and re-layouts  6.82 us (6%)
    pallas_call x1, Pallas kernels, whole(): pl.pallas_call(functools.partial(whole_kernel, nb), out_shape=(jax.ShapeD...  101 us
    pallas_call x1, Pallas kernels, place(): pl.pallas_call(functools.partial(place_kernel, nb), out_shape=jax.ShapeDt...  7.75 us
    unnamed x7, local copies, waits for them, and re-layouts  6.15 us

profile of v3, /device:TPU:3, one launch (start us, length us, event | category | flops | bytes accessed | tf_op | source)
XLA Modules:
  0.0 117.4 jit_solution(10152737776268003678)
XLA Ops:
  0.6 0.7 and_select_fusion.1
  1.3 0.7 pad.4.choice
  2.0 0.1 compare_convert_fusion.owned
  2.1 0.0 copy-start.1
  2.1 1.7 %copy-done.1 = bf16[1280,1024]{1,0:T(8,128)(2,1)S(1)} copy-done((bf16[1280,1024]{1,0:T(8,128)(2,1)S(1)}, bf16[1280,1024]{1,0:T(8,128)(2,1)}, u32[]{:S(2)}) %copy-start.1) | copy-done | bytes 2621464
  3.8 0.0 copy-start.2
  3.8 1.0 copy-done.2
  4.9 101.4 %shard_map.77 = (bf16[256,5120]{1,0:T(8,128)(2,1)S(1)}, bf16[4,2,2,64,1536]{4,3,2,1,0:T(8,128)(2,1)}, s32[4,4,8,128]{3,2,1,0:T(8,128)S(1)}) custom-call(s32[8,128]{1,0:T(8,128)S(1)} %pad.4.choice, bf16[128,16,1536]{2,1,0:T(8,128)(2,1)} %cat_in.1, bf16[2,2,2,160,1024]{4,3,2,1,0:T(8,128)(2,1)S(1)} %bitcast.5, bf16[256,5120]{1,0:T(8,128)(2,1)} %tokens_in.1, ...), custom_call_target="tpu_custom_call" | custom-call | tf_op jit(solution)/shard_map/pallas_call | solution.py:498
  106.3 0.0 copy-start
  106.3 1.9 %copy-done = bf16[4,2,2,64,1536]{4,3,2,1,0:T(8,128)(2,1)S(1)} copy-done((bf16[4,2,2,64,1536]{4,3,2,1,0:T(8,128)(2,1)S(1)}, bf16[4,2,2,64,1536]{4,3,2,1,0:T(8,128)(2,1)}, u32[]{:S(2)}) %copy-start) | copy-done | bytes 3145752
  108.2 7.8 %shard_map.78 = f32[128,16,1536]{2,1,0:T(8,128)} custom-call(s32[16,128]{1,0:T(8,128)S(1)} %bitcast.6, bf16[64,16,1536]{2,1,0:T(8,128)(2,1)S(1)} %bitcast.4), custom_call_target="tpu_custom_call" | custom-call | tf_op jit(solution)/shard_map/pallas_call | solution.py:572
  116.0 1.5 %copy.9 = bf16[256,5120]{1,0:T(8,128)(2,1)} copy(bf16[256,5120]{1,0:T(8,128)(2,1)S(1)} %get-tuple-element.10) | data formatting | bytes 5242880
  (2 shorter events, 0.0 us)
Async XLA Ops:
  2.1 1.7 %copy-start.1 = (bf16[1280,1024]{1,0:T(8,128)(2,1)S(1)}, bf16[1280,1024]{1,0:T(8,128)(2,1)}, u32[]{:S(2)}) copy-start(bf16[1280,1024]{1,0:T(8,128)(2,1)} %param.8) | copy-start | bytes 7864324
  3.8 1.0 copy-start.2
  106.3 1.9 %copy-start = (bf16[4,2,2,64,1536]{4,3,2,1,0:T(8,128)(2,1)S(1)}, bf16[4,2,2,64,1536]{4,3,2,1,0:T(8,128)(2,1)}, u32[]{:S(2)}) copy-start(bf16[4,2,2,64,1536]{4,3,2,1,0:T(8,128)(2,1)} %get-tuple-element.7) | copy-start | bytes 9437188

commit v4 on v3

--- a/solution.py
+++ b/solution.py
@@ -398,8 +398,11 @@
     fetched[me] = pieces[me, c, x]
     own.wait()
     freeze(me)
-    w_x(1).wait_recv()
-    w_y(1).start()
+
+    @pl.loop(1, nd)
+    def _(o):
+        w_x(o).wait_recv()
+        w_y(o).start()
 
     @pl.loop(1, nd)
     def _(o):
@@ -431,11 +434,6 @@
     mine.start()
     mine.wait()
     g_x(0).start()
-
-    @pl.loop(2, nd)
-    def _(o):
-        w_x(o).wait_recv()
-        w_y(o).start()
 
     @pl.loop(1, nd)
     def _(o):

time: 118 us -> 120 us (1.017); the launches traced: 117 us -> 117 us
  no operation moved by 1% of the time
where the time goes in v4:
time: 120 us; the launch traced here: 117 us
  Pallas kernels  109 us (91%)
  local copies, waits for them, and re-layouts  6.82 us (6%)
    pallas_call x1, Pallas kernels, whole(): pl.pallas_call(functools.partial(whole_kernel, nb), out_shape=(jax.ShapeD...  101 us
    pallas_call x1, Pallas kernels, place(): pl.pallas_call(functools.partial(place_kernel, nb), out_shape=jax.ShapeDt...  7.75 us
    unnamed x7, local copies, waits for them, and re-layouts  6.15 us

profile of v4, /device:TPU:3, one launch (start us, length us, event | category | flops | bytes accessed | tf_op | source)
XLA Modules:
  0.0 117.3 jit_solution(18077116256991172032)
XLA Ops:
  0.6 0.7 and_select_fusion.1
  1.3 0.7 pad.4.choice
  2.0 0.1 compare_convert_fusion.owned
  2.1 0.0 copy-start.1
  2.1 1.7 %copy-done.1 = bf16[1280,1024]{1,0:T(8,128)(2,1)S(1)} copy-done((bf16[1280,1024]{1,0:T(8,128)(2,1)S(1)}, bf16[1280,1024]{1,0:T(8,128)(2,1)}, u32[]{:S(2)}) %copy-start.1) | copy-done | bytes 2621464
  3.8 0.0 copy-start.2
  3.8 1.0 copy-done.2
  4.9 101.3 %shard_map.77 = (bf16[256,5120]{1,0:T(8,128)(2,1)S(1)}, bf16[4,2,2,64,1536]{4,3,2,1,0:T(8,128)(2,1)}, s32[4,4,8,128]{3,2,1,0:T(8,128)S(1)}) custom-call(s32[8,128]{1,0:T(8,128)S(1)} %pad.4.choice, bf16[128,16,1536]{2,1,0:T(8,128)(2,1)} %cat_in.1, bf16[2,2,2,160,1024]{4,3,2,1,0:T(8,128)(2,1)S(1)} %bitcast.5, bf16[256,5120]{1,0:T(8,128)(2,1)} %tokens_in.1, ...), custom_call_target="tpu_custom_call" | custom-call | tf_op jit(solution)/shard_map/pallas_call | solution.py:496
  106.2 0.0 copy-start
  106.2 1.9 %copy-done = bf16[4,2,2,64,1536]{4,3,2,1,0:T(8,128)(2,1)S(1)} copy-done((bf16[4,2,2,64,1536]{4,3,2,1,0:T(8,128)(2,1)S(1)}, bf16[4,2,2,64,1536]{4,3,2,1,0:T(8,128)(2,1)}, u32[]{:S(2)}) %copy-start) | copy-done | bytes 3145752
  108.1 7.7 %shard_map.78 = f32[128,16,1536]{2,1,0:T(8,128)} custom-call(s32[16,128]{1,0:T(8,128)S(1)} %bitcast.6, bf16[64,16,1536]{2,1,0:T(8,128)(2,1)S(1)} %bitcast.4), custom_call_target="tpu_custom_call" | custom-call | tf_op jit(solution)/shard_map/pallas_call | solution.py:570
  115.9 1.5 %copy.9 = bf16[256,5120]{1,0:T(8,128)(2,1)} copy(bf16[256,5120]{1,0:T(8,128)(2,1)S(1)} %get-tuple-element.10) | data formatting | bytes 5242880
  (2 shorter events, 0.0 us)
Async XLA Ops:
  2.1 1.7 %copy-start.1 = (bf16[1280,1024]{1,0:T(8,128)(2,1)S(1)}, bf16[1280,1024]{1,0:T(8,128)(2,1)}, u32[]{:S(2)}) copy-start(bf16[1280,1024]{1,0:T(8,128)(2,1)} %param.8) | copy-start | bytes 7864324
  3.8 1.0 copy-start.2
  106.2 1.9 %copy-start = (bf16[4,2,2,64,1536]{4,3,2,1,0:T(8,128)(2,1)S(1)}, bf16[4,2,2,64,1536]{4,3,2,1,0:T(8,128)(2,1)}, u32[]{:S(2)}) copy-start(bf16[4,2,2,64,1536]{4,3,2,1,0:T(8,128)(2,1)} %get-tuple-element.7) | copy-start | bytes 9437188

commit v5 on v3

--- a/solution.py
+++ b/solution.py
@@ -327,9 +327,8 @@
     def _(o):
         i_z(o).start()
 
-    @pl.loop(1, nd)
-    def _(o):
-        w_z(o).start()
+    w_z(1).start()
+    w_z(nd - 1).start()
 
     load_cat = pltpu.make_async_copy(cat_in, cat, local_sem.at[2])
     load_cat.start()
@@ -391,9 +390,15 @@
     def _(o):
         x_done(o)
         f_z(o).start()
-        w_z(o).wait_recv()
-        w_x(o).start()
-
+
+    @pl.loop(2, nd - 1)
+    def _(o):
+        w_z(o).start()
+
+    w_z(1).wait_recv()
+    w_x(1).start()
+    w_z(nd - 1).wait_recv()
+    w_x(nd - 1).start()
     x_done(0)
     fetched[me] = pieces[me, c, x]
     own.wait()
@@ -432,7 +437,15 @@
     mine.wait()
     g_x(0).start()
 
-    @pl.loop(2, nd)
+    w_x(nd - 1).wait_recv()
+    w_y(nd - 1).start()
+
+    @pl.loop(2, nd - 1)
+    def _(o):
+        w_z(o).wait_recv()
+        w_x(o).start()
+
+    @pl.loop(2, nd - 1)
     def _(o):
         w_x(o).wait_recv()
         w_y(o).start()
@@ -450,12 +463,17 @@
         g_x(o).wait_recv()
         g_c(o).start()
 
-    @pl.loop(2, nd)
+    w_y(nd - 1).wait_recv()
+    w_c(nd - 1).start()
+    w_c(1).wait_recv()
+    freeze(before(1))
+
+    @pl.loop(2, nd - 1)
     def _(o):
         w_y(o).wait_recv()
         w_c(o).start()
 
-    @pl.loop(1, nd)
+    @pl.loop(2, nd)
     def _(o):
         w_c(o).wait_recv()
         freeze(before(o))
@@ -597,7 +615,7 @@
     nd = lax.axis_size("dp")
     columns = block_count * rank
     owned = (element_slot_position // BLK)[:, None] == (jnp.arange(columns) // rank)[None, :]
-    if width % 128 == 0 and model_width // nd % 128 == 0:
+    if nd > 2 and width % 128 == 0 and model_width // nd % 128 == 0:
         choice = jnp.pad(segment_plugin_choice[None, :], ((0, 7), (0, 128 - block_count)))
         input_token_gradient, everyone, spread = whole(
             choice,

time: 118 us -> 112 us (0.949)
  Pallas kernels: 109 us -> 103 us
    pallas_call x1, Pallas kernels: 101 us -> 95.2 us  [whole(): pl.pallas_call(functools.partial(whole_kernel, nb), out_shape=(jax.ShapeD...]
where the time goes in v5:
time: 112 us; the launch traced here: 111 us
  Pallas kernels  103 us (92%)
  local copies, waits for them, and re-layouts  6.82 us (6%)
    pallas_call x1, Pallas kernels, whole(): pl.pallas_call(functools.partial(whole_kernel, nb), out_shape=(jax.ShapeD...  95.2 us
    pallas_call x1, Pallas kernels, place(): pl.pallas_call(functools.partial(place_kernel, nb), out_shape=jax.ShapeDt...  7.74 us
    unnamed x7, local copies, waits for them, and re-layouts  6.15 us

profile of v5, /device:TPU:3, one launch (start us, length us, event | category | flops | bytes accessed | tf_op | source)
XLA Modules:
  0.0 111.2 jit_solution(7544202698435268287)
XLA Ops:
  0.6 0.7 and_select_fusion.1
  1.3 0.7 pad.4.choice
  2.0 0.1 compare_convert_fusion.owned
  2.1 0.0 copy-start.1
  2.1 1.7 %copy-done.1 = bf16[1280,1024]{1,0:T(8,128)(2,1)S(1)} copy-done((bf16[1280,1024]{1,0:T(8,128)(2,1)S(1)}, bf16[1280,1024]{1,0:T(8,128)(2,1)}, u32[]{:S(2)}) %copy-start.1) | copy-done | bytes 2621464
  3.8 0.0 copy-start.2
  3.8 1.0 copy-done.2
  4.9 95.2 %shard_map.77 = (bf16[256,5120]{1,0:T(8,128)(2,1)S(1)}, bf16[4,2,2,64,1536]{4,3,2,1,0:T(8,128)(2,1)}, s32[4,4,8,128]{3,2,1,0:T(8,128)S(1)}) custom-call(s32[8,128]{1,0:T(8,128)S(1)} %pad.4.choice, bf16[128,16,1536]{2,1,0:T(8,128)(2,1)} %cat_in.1, bf16[2,2,2,160,1024]{4,3,2,1,0:T(8,128)(2,1)S(1)} %bitcast.5, bf16[256,5120]{1,0:T(8,128)(2,1)} %tokens_in.1, ...), custom_call_target="tpu_custom_call" | custom-call | tf_op jit(solution)/shard_map/pallas_call | solution.py:516
  100.1 0.0 copy-start
  100.1 1.9 %copy-done = bf16[4,2,2,64,1536]{4,3,2,1,0:T(8,128)(2,1)S(1)} copy-done((bf16[4,2,2,64,1536]{4,3,2,1,0:T(8,128)(2,1)S(1)}, bf16[4,2,2,64,1536]{4,3,2,1,0:T(8,128)(2,1)}, u32[]{:S(2)}) %copy-start) | copy-done | bytes 3145752
  102.0 7.7 %shard_map.78 = f32[128,16,1536]{2,1,0:T(8,128)} custom-call(s32[16,128]{1,0:T(8,128)S(1)} %bitcast.6, bf16[64,16,1536]{2,1,0:T(8,128)(2,1)S(1)} %bitcast.4), custom_call_target="tpu_custom_call" | custom-call | tf_op jit(solution)/shard_map/pallas_call | solution.py:590
  109.8 1.5 %copy.9 = bf16[256,5120]{1,0:T(8,128)(2,1)} copy(bf16[256,5120]{1,0:T(8,128)(2,1)S(1)} %get-tuple-element.10) | data formatting | bytes 5242880
  (2 shorter events, 0.0 us)
Async XLA Ops:
  2.1 1.7 %copy-start.1 = (bf16[1280,1024]{1,0:T(8,128)(2,1)S(1)}, bf16[1280,1024]{1,0:T(8,128)(2,1)}, u32[]{:S(2)}) copy-start(bf16[1280,1024]{1,0:T(8,128)(2,1)} %param.8) | copy-start | bytes 7864324
  3.8 1.0 copy-start.2
  100.1 1.9 %copy-start = (bf16[4,2,2,64,1536]{4,3,2,1,0:T(8,128)(2,1)S(1)}, bf16[4,2,2,64,1536]{4,3,2,1,0:T(8,128)(2,1)}, u32[]{:S(2)}) copy-start(bf16[4,2,2,64,1536]{4,3,2,1,0:T(8,128)(2,1)} %get-tuple-element.7) | copy-start | bytes 9437188
